TPU v7x, 32 devices: a whole 2x2x4 slice. The times are simulated.
32 devices in a mesh: ctx: 4 (over y, x), tp: 8 (over z, core).
Axes of the slice: x: 2, y: 2, z: 4, core: 2. Of those that a mesh axis runs over, the one named last changes fastest.
Arguments:
- tokens: bfloat16 [4096, 2560], P(('ctx', 'tp')), may hold values from -8 to 8
- norm1_gain: float32 [2560], replicated, may hold values from 0.1 to 1.9
- w_z: bfloat16 [2560, 5120], P(None, 'tp'), may hold values from -0.125 to 0.125
- w_x: bfloat16 [2560, 5120], P(None, 'tp'), may hold values from -0.125 to 0.125
- w_bc: bfloat16 [2560, 256], replicated, may hold values from -0.125 to 0.125
- w_dt: bfloat16 [2560, 80], P(None, 'tp'), may hold values from -1 to 1
- dt_bias: float32 [80], P('tp'), may hold values from -5.5 to -4
- a_log: float32 [80], P('tp'), may hold values from -12 to 1.4
- conv_x: float32 [4, 5120], P(None, 'tp'), may hold values from -3 to 3
- conv_bc: float32 [4, 256], replicated, may hold values from -3 to 3
- d_skip: float32 [80], P('tp'), may hold values from 0.1 to 1.9
- ssm_gain: float32 [5120], P('tp'), may hold values from 0.1 to 1.9
- w_out: bfloat16 [5120, 2560], P('tp'), may hold values from -0.078125 to 0.078125
- norm2_gain: float32 [2560], replicated, may hold values from 0.1 to 1.9
- w_gate: bfloat16 [2560, 5120], P(None, 'tp'), may hold values from -0.125 to 0.125
- w_up: bfloat16 [2560, 5120], P(None, 'tp'), may hold values from -0.125 to 0.125
- w_down: bfloat16 [5120, 2560], P('tp'), may hold values from -0.078125 to 0.078125
Outputs:
- layer_out: bfloat16 [4096, 2560], P(('ctx', 'tp'))
All inputs are finite; a program needn't handle non-finite values.
Results may differ from a plain program's by a relative error of at most 0.017.
Values may be sent and summed in bfloat16 or wider, within the bound.
A program may use at most 128 MiB of HBM per device.

v0:
```python
import jax
import jax.numpy as jnp
from jax import lax
from jax.sharding import PartitionSpec as P

HEADS = 80
HEAD_DIM = 64
STATE_DIM = 128
BLOCK_LEN = 256


EPS = 1e-05


def from_behind(value, axis, steps):
    count = lax.axis_size(axis)
    first, last = (max(0, -steps), min(count, count - steps))
    return lax.ppermute(value, axis, [(source, source + steps) for source in range(first, last)])


def carried_in(shard, axis, join, neutral):
    place = lax.axis_index(axis)
    gathered = jax.tree.map(
        lambda a, kind: lax.all_gather(a.astype(kind), axis), shard, (jnp.bfloat16, jnp.bfloat16)
    )
    state = jax.tree.map(lambda a, e: jnp.zeros_like(a) + jnp.asarray(e, a.dtype), shard, neutral)

    def one(step, state):
        return join(
            state,
            jax.tree.map(
                lambda a, own: lax.dynamic_index_in_dim(a, step, 0, False).astype(own.dtype),
                gathered,
                shard,
            ),
        )

    return lax.fori_loop(0, place, one, state)


def rms_rows(values, gain):
    wide = values.astype(jnp.float32)
    return wide * lax.rsqrt(jnp.mean(wide * wide, axis=-1, keepdims=True) + EPS) * gain


def conv_four(rim, current, kernel):
    extended = jnp.concatenate([rim, current], axis=0).astype(jnp.float32)
    length = current.shape[0]
    result = kernel[0] * extended[0:length]
    for offset in range(1, 4):
        result = result + kernel[offset] * extended[offset : offset + length]
    return result


def combine_states(prior_part, next_part):
    return (
        prior_part[0] * next_part[0],
        next_part[1] + next_part[0][:, None, None] * prior_part[1],
    )


def carry_step(state, pieces):
    decay_now, fresh = pieces
    return (decay_now[:, None, None] * state + fresh, state)


def local(
    tokens,
    norm1_gain,
    w_z,
    w_x,
    w_bc,
    w_dt,
    dt_bias,
    a_log,
    conv_x,
    conv_bc,
    d_skip,
    ssm_gain,
    w_out,
    norm2_gain,
    w_gate,
    w_up,
    w_down,
):
    gathered = lax.all_gather(tokens, "tp", axis=0, tiled=True)
    normed = rms_rows(gathered, norm1_gain).astype(jnp.bfloat16)
    bc_rows = jnp.dot(normed, w_bc, preferred_element_type=jnp.float32).astype(jnp.bfloat16)
    group_len = gathered.shape[0]
    head_count = w_dt.shape[1]
    channels = w_x.shape[1]
    gate_z = jnp.dot(normed, w_z, preferred_element_type=jnp.float32)
    inner_rows = jnp.dot(normed, w_x, preferred_element_type=jnp.float32).astype(jnp.bfloat16)
    dt_raw = jnp.dot(normed, w_dt, preferred_element_type=jnp.float32)
    rim_inner, rim_bc = from_behind((inner_rows[-3:], bc_rows[-3:]), "ctx", 1)
    conv_inner = jax.nn.silu(conv_four(rim_inner, inner_rows, conv_x)).astype(jnp.bfloat16)
    conv_bcm = jax.nn.silu(conv_four(rim_bc, bc_rows, conv_bc)).astype(jnp.bfloat16)
    dt_step = jax.nn.softplus(dt_raw + dt_bias)
    log_decay = -dt_step * jnp.exp(a_log)
    block_count = group_len // BLOCK_LEN
    log_blocks = log_decay.reshape(block_count, BLOCK_LEN, head_count)
    step_blocks = dt_step.reshape(block_count, BLOCK_LEN, head_count)
    cum_decay = jnp.cumsum(log_blocks, axis=1)
    b_mat = conv_bcm[:, :STATE_DIM].reshape(block_count, BLOCK_LEN, STATE_DIM)
    c_mat = conv_bcm[:, STATE_DIM:].reshape(block_count, BLOCK_LEN, STATE_DIM)
    scores = jnp.einsum("btn,bsn->bts", c_mat, b_mat, preferred_element_type=jnp.float32)
    causal_mask = jnp.tril(jnp.ones((BLOCK_LEN, BLOCK_LEN), dtype=bool))[None, :, :, None]
    decay_diff = jnp.where(causal_mask, cum_decay[:, :, None, :] - cum_decay[:, None, :, :], 0.0)
    weights = jnp.where(causal_mask, jnp.exp(decay_diff), 0.0)
    inner_wide = conv_inner.astype(jnp.float32).reshape(
        block_count, BLOCK_LEN, head_count, HEAD_DIM
    )
    scaled = inner_wide * step_blocks[..., None]
    mixed_w = scores[..., None] * weights
    y_intra = jnp.einsum("btsh,bshp->bthp", mixed_w, scaled, precision=lax.Precision.HIGHEST)
    block_last = cum_decay[:, -1, :]
    tail_decay = jnp.exp(block_last[:, None, :] - cum_decay)
    b_wide = b_mat.astype(jnp.float32)
    c_wide = c_mat.astype(jnp.float32)
    block_states = jnp.einsum(
        "bsh,bshp,bsn->bhpn", tail_decay, scaled, b_wide, precision=lax.Precision.HIGHEST
    )
    block_decay = jnp.exp(block_last)
    zero_state = jnp.zeros((head_count, HEAD_DIM, STATE_DIM), jnp.float32)
    local_final, local_in = lax.scan(carry_step, zero_state, (block_decay, block_states))
    total_decay = jnp.prod(block_decay, axis=0)
    prior_decay = jnp.exp(jnp.cumsum(block_last, axis=0) - block_last)
    identity = (jnp.ones((head_count,), jnp.float32), zero_state)
    incoming_decay, incoming = carried_in(
        (total_decay, local_final), "ctx", combine_states, identity
    )
    state_in = local_in + prior_decay[:, :, None, None] * incoming[None]
    y_inter = jnp.exp(cum_decay)[..., None] * jnp.einsum(
        "btn,bhpn->bthp", c_wide, state_in, precision=lax.Precision.HIGHEST
    )
    ssm_out = y_intra + y_inter + d_skip[None, None, :, None] * inner_wide
    gated = ssm_out.reshape(group_len, channels) * jax.nn.silu(gate_z)
    squares = lax.psum(jnp.sum(gated * gated, axis=-1), "tp")
    scaled_out = (gated * lax.rsqrt(squares / (HEADS * HEAD_DIM) + EPS)[:, None] * ssm_gain).astype(
        jnp.bfloat16
    )
    piece = scaled_out
    mixer_own = lax.psum_scatter(
        jnp.dot(piece, w_out, preferred_element_type=jnp.float32).astype(jnp.bfloat16),
        "tp",
        scatter_dimension=0,
        tiled=True,
    ).astype(jnp.float32)
    resid = (tokens.astype(jnp.float32) + mixer_own).astype(jnp.bfloat16)
    normed_own = rms_rows(resid, norm2_gain).astype(jnp.bfloat16)
    mlp_in = lax.all_gather(normed_own, "tp", axis=0, tiled=True)
    mlp_gate = jnp.dot(mlp_in, w_gate, preferred_element_type=jnp.float32)
    mlp_up = jnp.dot(mlp_in, w_up, preferred_element_type=jnp.float32)
    hidden = (jax.nn.silu(mlp_gate) * mlp_up).astype(jnp.bfloat16)
    piece = hidden
    mlp_down = lax.psum_scatter(
        jnp.dot(piece, w_down, preferred_element_type=jnp.float32).astype(jnp.bfloat16),
        "tp",
        scatter_dimension=0,
        tiled=True,
    ).astype(jnp.float32)
    return (resid.astype(jnp.float32) + mlp_down).astype(jnp.bfloat16)


def solution(mesh):
    return jax.shard_map(
        local,
        mesh=mesh,
        in_specs=(
            P(("ctx", "tp"), None),
            P(),
            P(None, "tp"),
            P(None, "tp"),
            P(),
            P(None, "tp"),
            P("tp"),
            P("tp"),
            P(None, "tp"),
            P(),
            P("tp"),
            P("tp"),
            P("tp", None),
            P(),
            P(None, "tp"),
            P(None, "tp"),
            P("tp", None),
        ),
        out_specs=P(("ctx", "tp"), None),
        check_vma=False,
    )
```

profile of v0, /device:TPU:0, one launch (start us, length us, event | category | flops | bytes accessed | tf_op | source)
XLA Modules:
  0.0 434.6 jit_solution(16150217493584793742)
XLA Ops:
  13.0 54.8 %all-gather.5.cloned.1.call-done = bf16[1024,2560]{1,0:T(8,128)(2,1)} async-done(((bf16[128,2560]{1,0:T(8,128)(2,1)}), bf16[1024,2560]{1,0:T(8,128)(2,1)}) %all-gather.5.cloned.1.call-update) | async-done | bytes 5242896 | tf_op jit(solution)/shard_map/all_gather | solution.py:86
  67.8 3.7 fusion.1
  78.2 4.6 %convolution_convert_fusion.3 = bf16[1024,256]{1,0:T(8,128)(2,1)S(1)} fusion(bf16[2560,256]{1,0:T(8,128)(2,1)} %param.25, bf16[1024,2560]{1,0:T(8,128)(2,1)} %all-gather.5.cloned.1.call-done, f32[2560]{0:T(1024)} %param.22, f32[1024]{0:T(1024)S(1)} %add_rsqrt_fusion.1), kind=kOutput, calls=%fused_computation.59 | convolution fusion | flops 1352925184 | bytes 7092224 | tf_op jit(solution)/shard_map/dot_general | solution.py:88
  83.6 3.5 collective-permute-start.1
  87.1 6.8 %convolution_convert_fusion.2 = bf16[1024,640]{1,0:T(8,128)(2,1)S(1)} fusion(bf16[2560,640]{1,0:T(8,128)(2,1)S(1)} %copy-done.17, bf16[1024,2560]{1,0:T(8,128)(2,1)} %all-gather.5.cloned.1.call-done, f32[2560]{0:T(1024)S(1)} %copy-done.19, f32[1024]{0:T(1024)S(1)} %add_rsqrt_fusion.1), kind=kOutput, calls=%fused_computation.45 | convolution fusion | flops 3366584320 | bytes 9844736 | tf_op jit(solution)/shard_map/dot_general | solution.py:93
  96.0 4.0 collective-permute-start
  100.0 8.9 %all-reduce = bf16[40]{0:T(256)(128)(2,1)S(1)} all-reduce(bf16[40]{0:T(256)(128)(2,1)S(1)} %dynamic-update-slice), channel_id=3, replica_groups=mesh['ctx'=4,'tp'=8] {'ctx'}, use_global_device_ids=true, to_apply=%add | all-reduce | flops 40 | bytes 160
  115.0 3.0 fusion.30
  118.0 3.3 copy.47
  121.3 4.2 reshape.107
  125.5 4.2 broadcast_multiply_fusion
  129.7 2.7 fusion.19
  132.4 16.1 %while.26 = (s32[]{:T(128)}, f32[10,64,128]{2,1,0:T(8,128)}, f32[4,10,64,128]{3,2,1,0:T(8,128)}, f32[4,10]{1,0:T(4,128)}, f32[4,10,64,128]{3,2,1,0:T(8,128)}, /*index=5*/s32[]{:T(128)}, s32[]{:T(128)}) while((s32[]{:T(128)}, f32[10,64,128]{2,1,0:T(8,128)}, f32[4,10,64,128]{3,2,1,0:T(8,128)}, f32[4,10]{1,0:T(4,128)}, ...), condition=%wide.region_4.5_spmd.clone, body=%wide.region_3.4_spmd.clone.sunk | while | flops 327683 | bytes 1639128 | solution.py:125
  149.4 12.0 %all-gather = bf16[40,64,128]{2,1,0:T(8,128)(2,1)} all-gather(bf16[10,64,128]{2,1,0:T(8,128)(2,1)S(1)} %convert_element_type.104), channel_id=2, replica_groups=mesh['ctx'=4,'tp'=8] {'ctx'}, dimensions={0}, use_global_device_ids=true | all-gather | bytes 819200 | tf_op jit(solution)/shard_map/all_gather | solution.py:24
  162.4 13.9 %fusion.4 = f32[4,10,64,256]{3,2,1,0:T(8,128)S(1)} fusion(f32[4,256,10]{1,2,0:T(8,128)} %copy.52, f32[4,256,256]{2,1,0:T(8,128)} %fusion.48, pred[256,256]{1,0:T(8,128)(4,1)} %iota_compare_fusion, f32[4,256,10,64]{1,0,3,2:T(4,128)} %get-tuple-element.123), kind=kOutput, calls=%fused_computation.11 | convolution fusion | flops 2023751680 | bytes 6397952 | tf_op jit(solution)/shard_map/btsh,bshp->bthp/dot_general | solution.py:115
  181.9 3.4 copy.63
  185.3 10.2 %multiply_reduce_fusion = (f32[1024]{0:T(1024)S(1)}, f32[1024,640]{1,0:T(8,128)}) fusion(f32[1024,640]{1,0:T(8,128)} %copy.63, bf16[2560,640]{1,0:T(8,128)(2,1)} %param.23, bf16[1024,2560]{1,0:T(8,128)(2,1)} %all-gather.5.cloned.1.call-done, f32[2560]{0:T(1024)S(1)} %copy-done.20, f32[1024]{0:T(1024)S(1)} %copy-done.14), kind=kOutput, calls=%fused_computation.39 | convolution fusion | flops 3370515456 | bytes 13780992 | tf_op jit(solution)/shard_map/dot_general | solution.py:92
  195.5 13.6 %psum.7 = f32[1024]{0:T(1024)S(1)} all-reduce(f32[1024]{0:T(1024)S(1)} %get-tuple-element.137), channel_id=1, replica_groups=mesh['ctx'=4,'tp'=8] {'tp'}, use_global_device_ids=true, to_apply=%region_10.11 | all-reduce | flops 1024 | bytes 8192 | tf_op jit(solution)/shard_map/psum | solution.py:138
  209.2 9.6 %convolution_convert_fusion.1 = bf16[1024,2560]{1,0:T(8,128)(2,1)} fusion(bf16[640,2560]{1,0:T(8,128)(2,1)S(1)} %copy-done, f32[640]{0:T(1024)S(1)} %copy-done.21, f32[1024]{0:T(1024)S(1)} %add_rsqrt_fusion, f32[1024,640]{1,0:T(8,128)} %copy.63, f32[1024,640]{1,0:T(8,128)} %get-tuple-element.138), kind=kOutput, calls=%fused_computation.18 | convolution fusion | flops 3363307520 | bytes 13769216 | tf_op jit(solution)/shard_map/dot_general | solution.py:144
  218.8 62.8 %reduce-scatter.3.cloned.1.call-done = bf16[128,2560]{1,0:T(8,128)(2,1)} async-done(((bf16[1024,2560]{1,0:T(8,128)(2,1)}), bf16[128,2560]{1,0:T(8,128)(2,1)}) %reduce-scatter.3.cloned.1.call-update) | async-done | bytes 655376 | tf_op jit(solution)/shard_map/reduce_scatter | solution.py:143
  285.7 54.5 %all-gather.7.cloned.1.call-done = bf16[1024,2560]{1,0:T(8,128)(2,1)} async-done(((bf16[128,2560]{1,0:T(8,128)(2,1)}), bf16[1024,2560]{1,0:T(8,128)(2,1)}) %all-gather.7.cloned.1.call-update) | async-done | bytes 5242896 | tf_op jit(solution)/shard_map/all_gather | solution.py:151
  340.2 9.2 %fusion.49 = f32[1024,640]{1,0:T(8,128)} fusion(bf16[1024,2560]{1,0:T(8,128)(2,1)} %all-gather.7.cloned.1.call-done, bf16[2560,640]{1,0:T(8,128)(2,1)} %param.35), kind=kOutput, calls=%fused_computation.96 | convolution fusion | flops 3355443200 | bytes 11141120 | tf_op jit(solution)/shard_map/dot_general | solution.py:152
  349.4 17.0 %convolution_convert_fusion = bf16[1024,2560]{1,0:T(8,128)(2,1)} fusion(bf16[640,2560]{1,0:T(8,128)(2,1)} %param.37, f32[1024,640]{1,0:T(8,128)} %fusion.49, bf16[1024,2560]{1,0:T(8,128)(2,1)} %all-gather.7.cloned.1.call-done, bf16[2560,640]{1,0:T(8,128)(2,1)} %param.36), kind=kOutput, calls=%fused_computation.17 | convolution fusion | flops 6717440000 | bytes 19660800 | tf_op jit(solution)/shard_map/dot_general | solution.py:157
  366.4 58.8 %reduce-scatter.5.cloned.1.call-done = bf16[128,2560]{1,0:T(8,128)(2,1)} async-done(((bf16[1024,2560]{1,0:T(8,128)(2,1)}), bf16[128,2560]{1,0:T(8,128)(2,1)}) %reduce-scatter.5.cloned.1.call-update) | async-done | bytes 655376 | tf_op jit(solution)/shard_map/reduce_scatter | solution.py:156
  (121 shorter events, 51.5 us)
Async XLA Ops:
  6.5 202.6 %copy-start = (bf16[640,2560]{1,0:T(8,128)(2,1)S(1)}, bf16[640,2560]{1,0:T(8,128)(2,1)}, u32[]{:S(2)}) copy-start(bf16[640,2560]{1,0:T(8,128)(2,1)} %param.33) | copy-start | bytes 9830404
  6.5 61.2 %all-gather.5.cloned.1.call-start = ((), (), s32[]{:S(2)}) async-start(), calls=%async_computation.2 | async-start | bytes 5898240 | tf_op jit(solution)/shard_map/all_gather | solution.py:86
  7.3 274.4 %reduce-scatter.3.cloned.1.call-start = ((), (), s32[]{:S(2)}) async-start(), calls=%async_computation.3 | async-start | bytes 5898240 | tf_op jit(solution)/shard_map/reduce_scatter | solution.py:143
  11.6 59.9 %copy-start.22 = (f32[10]{0:T(128)S(1)}, f32[10]{0:T(128)}, u32[]{:S(2)}) copy-start(f32[10]{0:T(128)} %param.27) | copy-start | bytes 124
  13.0 58.5 %copy-start.18 = (f32[2560]{0:T(1024)S(1)}, f32[2560]{0:T(1024)}, u32[]{:S(2)}) copy-start(f32[2560]{0:T(1024)} %param.22) | copy-start | bytes 30724
  67.8 4.0 copy-start.3
  71.8 15.3 %copy-start.13 = (f32[1024]{0:T(1024)}, f32[1024]{0:T(1024)S(1)}, u32[]{:S(2)}) copy-start(f32[1024]{0:T(1024)S(1)} %add_rsqrt_fusion.1) | copy-start | bytes 12292
  78.2 8.9 %copy-start.17 = (bf16[2560,640]{1,0:T(8,128)(2,1)S(1)}, bf16[2560,640]{1,0:T(8,128)(2,1)}, u32[]{:S(2)}) copy-start(bf16[2560,640]{1,0:T(8,128)(2,1)} %param.24) | copy-start | bytes 9830404
  78.2 8.9 %copy-start.19 = (f32[2560]{0:T(1024)S(1)}, f32[2560]{0:T(1024)}, u32[]{:S(2)}) copy-start(f32[2560]{0:T(1024)} %param.22) | copy-start | bytes 30724
  83.6 28.4 %copy-start.15 = (f32[1,256]{1,0:T(1,128)S(1)}, f32[1,256]{1,0:T(1,128)}, u32[]{:S(2)}) copy-start(f32[1,256]{1,0:T(1,128)} %get-tuple-element.131) | copy-start | bytes 3076
  83.6 27.2 %collective-permute-start.1 = (bf16[3,256]{1,0:T(4,128)(2,1)S(1)}, bf16[3,256]{1,0:T(4,128)(2,1)S(1)}, u32[]{:S(2)}, u32[]{:S(2)}) collective-permute-start(bf16[3,256]{1,0:T(4,128)(2,1)S(1)} %slice.97), channel_id=1, source_target_pairs={{0,8},{8,16},{16,24},{1,9},{9,17},{17,25},{2,10},{10,18},{18,26},{... | collective-permute-start | bytes 4616 | tf_op jit(solution)/shard_map/ppermute | solution.py:18
  96.0 18.0 %collective-permute-start = (bf16[3,640]{1,0:T(4,128)(2,1)}, bf16[3,640]{1,0:T(4,128)(2,1)}, u32[]{:S(2)}, u32[]{:S(2)}) collective-permute-start(bf16[3,640]{1,0:T(4,128)(2,1)} %slice.92), channel_id=1, source_target_pairs={{0,8},{8,16},{16,24},{1,9},{9,17},{17,25},{2,10},{10,18},{18,26},{... | collective-permute-start | bytes 11528 | tf_op jit(solution)/shard_map/ppermute | solution.py:18
  125.5 4.2 copy-start.5
  132.4 29.8 %copy-start.23 = (bf16[4,10]{1,0:T(4,128)(2,1)S(1)}, bf16[4,10]{1,0:T(4,128)(2,1)}, u32[]{:S(2)}) copy-start(bf16[4,10]{1,0:T(4,128)(2,1)} %reshape.109) | copy-start | bytes 244
  162.3 13.9 %copy-start.1 = (f32[4,256,10,64]{1,0,3,2:T(4,128)S(1)}, f32[4,256,10,64]{1,0,3,2:T(4,128)}, u32[]{:S(2)}) copy-start(f32[4,256,10,64]{1,0,3,2:T(4,128)} %reshape.107) | copy-start | bytes 7864324
  162.3 13.9 %copy-start.2 = (f32[10,64,128]{2,1,0:T(8,128)S(1)}, f32[10,64,128]{2,1,0:T(8,128)}, u32[]{:S(2)}) copy-start(f32[10,64,128]{2,1,0:T(8,128)} %get-tuple-element.79) | copy-start | bytes 983044
  162.3 13.9 %copy-start.8 = (f32[4,10,64,128]{3,2,1,0:T(8,128)S(1)}, f32[4,10,64,128]{3,2,1,0:T(8,128)}, u32[]{:S(2)}) copy-start(f32[4,10,64,128]{3,2,1,0:T(8,128)} %get-tuple-element.77) | copy-start | bytes 3932164
  162.3 13.9 %copy-start.10 = (f32[4,256,10]{1,2,0:T(8,128)S(1)}, f32[4,256,10]{1,2,0:T(8,128)}, u32[]{:S(2)}) copy-start(f32[4,256,10]{1,2,0:T(8,128)} %copy.55) | copy-start | bytes 122884
  162.4 13.9 %copy-start.12 = (f32[4,10]{1,0:T(4,128)S(1)}, f32[4,10]{1,0:T(4,128)}, u32[]{:S(2)}) copy-start(f32[4,10]{1,0:T(4,128)} %get-tuple-element.132) | copy-start | bytes 484
  162.4 13.9 %copy-start.16 = (f32[10]{0:T(128)S(1)}, f32[10]{0:T(128)}, u32[]{:S(2)}) copy-start(f32[10]{0:T(128)} %param.31) | copy-start | bytes 124
  185.3 23.8 %copy-start.21 = (f32[640]{0:T(1024)S(1)}, f32[640]{0:T(1024)}, u32[]{:S(2)}) copy-start(f32[640]{0:T(1024)} %param.32) | copy-start | bytes 7684
  218.8 64.5 %copy-start.11 = (f32[2560]{0:T(1024)S(1)}, f32[2560]{0:T(1024)}, u32[]{:S(2)}) copy-start(f32[2560]{0:T(1024)} %param.34) | copy-start | bytes 30724
  218.8 121.4 %all-gather.7.cloned.1.call-start = ((), (), s32[]{:S(2)}) async-start(), calls=%async_computation.4 | async-start | bytes 5898240 | tf_op jit(solution)/shard_map/all_gather | solution.py:151
  285.6 139.6 %reduce-scatter.5.cloned.1.call-start = ((), (), s32[]{:S(2)}) async-start(), calls=%async_computation.5 | async-start | bytes 5898240 | tf_op jit(solution)/shard_map/reduce_scatter | solution.py:156
  (6 other events, 12.3 us)
Sparse Core Ops, SparseCore 0:
  9.0 58.7 all-gather.4
  218.9 62.6 reduce-scatter.2
  285.8 54.3 all-gather.6
  366.5 58.6 reduce-scatter.4
where the time goes:
time: 442 us; the launch traced here: 435 us
  waiting for transfers between devices  232 us (52%)
  matrix products  79.5 us (18%)
  other arithmetic  39 us (9%)
  blocking collectives  34.5 us (8%)
  local copies, waits for them, and re-layouts  27.7 us (6%)
  between operations  14.5 us (3%)
  starting transfers between devices  7.57 us (2%)
    reduce_scatter x1, waiting for transfers between devices, local(): lax.psum_scatter(jnp.dot(piece, w_out, preferred_element_type=jnp.float32...  62.8 us
    reduce_scatter x1, waiting for transfers between devices, local(): lax.psum_scatter(jnp.dot(piece, w_down, preferred_element_type=jnp.float3...  58.8 us
    all_gather x1, waiting for transfers between devices, local(): gathered = lax.all_gather(tokens, 'tp', axis=0, tiled=True)  54.8 us
    all_gather x1, waiting for transfers between devices, local(): mlp_in = lax.all_gather(normed_own, 'tp', axis=0, tiled=True)  54.5 us
    dot_general x1, matrix products, local(): jnp.dot(piece, w_down, preferred_element_type=jnp.float32)  17 us
    dot_general x1, matrix products, local(): jnp.einsum('btsh,bshp->bthp', mixed_w, scaled, precision=lax.Precision.HI...  13.9 us
    psum x1, blocking collectives, local(): squares = lax.psum(jnp.sum(gated * gated, axis=-1), 'tp')  13.6 us
    all_gather x1, blocking collectives, carried_in(): lax.all_gather(a.astype(kind), axis)  12 us
  transfers between devices with their start and end apart: 6, of which 4 were waited for; matrix products, arithmetic and copies ran while one was open for 4% of the time, Pallas kernels for 0%

commit v1 on v0

v1 whole, which is shorter than its diff:
```python
import functools

import jax
import jax.numpy as jnp
from jax import lax
from jax.experimental import pallas as pl
from jax.experimental.pallas import tpu as pltpu
from jax.sharding import PartitionSpec as P

HEADS = 80
HEAD_DIM = 64
STATE_DIM = 128
BLOCK_LEN = 256
EPS = 1e-05
F32 = jnp.float32
BF16 = jnp.bfloat16
MESH = pl.DeviceIdType.MESH
VMEM_LIMIT = 60 * 1024 * 1024


def from_behind(value, axis, steps):
    count = lax.axis_size(axis)
    first, last = (max(0, -steps), min(count, count - steps))
    return lax.ppermute(value, axis, [(source, source + steps) for source in range(first, last)])


def rms_rows(values, gain):
    wide = values.astype(F32)
    return wide * lax.rsqrt(jnp.mean(wide * wide, axis=-1, keepdims=True) + EPS) * gain


def conv_four(rim, current, kernel):
    extended = jnp.concatenate([rim, current], axis=0).astype(F32)
    length = current.shape[0]
    result = kernel[0] * extended[0:length]
    for offset in range(1, 4):
        result = result + kernel[offset] * extended[offset : offset + length]
    return result


def silu(x):
    return x / (1.0 + jnp.exp(-x))


def place():
    me = lax.axis_index("tp")
    return me, me // 2, me % 2


def greet(peers, number):
    barrier = pltpu.get_barrier_semaphore()
    for cond, peer in peers:

        @pl.when(cond)
        def _():
            pl.semaphore_signal(barrier, inc=1, device_id={"tp": peer}, device_id_type=MESH)

    pl.semaphore_wait(barrier, number)


def remote(src, dst, send, recv, peer):
    return pltpu.make_async_remote_copy(
        src_ref=src, dst_ref=dst, send_sem=send, recv_sem=recv,
        device_id={"tp": peer}, device_id_type=MESH,
    )


class Gather:
    def __init__(self, held, sems, chips, rows):
        self.held, self.sems, self.chips, self.rows = held, sems, chips, rows
        self.me, self.z, self.c = place()

    def half(self, chip, core):
        return self.held.at[chip, pl.ds(pl.multiple_of(core * self.rows, 16), self.rows)]

    def copy(self, kind, chip, core):
        send, recv = self.sems
        peer = (self.me + 2, self.me - 2, self.z * 2 + 1 - self.c)[kind]
        part = self.half(chip, core)
        return remote(part, part, send.at[kind, chip], recv.at[kind, chip], peer)

    def start(self):
        @pl.when(self.z < self.chips - 1)
        def _():
            self.copy(0, self.z, self.c).start()

        @pl.when(self.z > 0)
        def _():
            self.copy(1, self.z, self.c).start()

        self.copy(2, self.z, self.c).start()

    def arrive(self, step):
        below, above = self.z - 1 - step, self.z + 1 + step

        @pl.when(below >= 0)
        def _():
            self.copy(0, below, self.c).wait_recv()

            @pl.when(self.z < self.chips - 1)
            def _():
                self.copy(0, below, self.c).start()

            self.copy(2, below, self.c).start()

        @pl.when(above < self.chips)
        def _():
            self.copy(1, above, self.c).wait_recv()

            @pl.when(self.z > 0)
            def _():
                self.copy(1, above, self.c).start()

            self.copy(2, above, self.c).start()

    def both(self, chip):
        self.copy(2, chip, 1 - self.c).wait_recv()

    def finish(self):
        @pl.loop(0, self.chips)
        def _(chip):
            @pl.when((chip <= self.z) & (self.z < self.chips - 1))
            def _():
                self.copy(0, chip, self.c).wait_send()

            @pl.when((chip >= self.z) & (self.z > 0))
            def _():
                self.copy(1, chip, self.c).wait_send()

            self.copy(2, chip, self.c).wait_send()


def project_kernel(
    chips, rows, tok, gain, w_z, w_x, w_bc, w_dt, z_out, x_out, bc_out, dt_out, held, send, recv
):
    me, z, c = place()
    greet(
        [(z < chips - 1, me + 2), (z > 0, me - 2), (z >= 0, z * 2 + 1 - c)],
        1 + (z < chips - 1).astype(jnp.int32) + (z > 0).astype(jnp.int32),
    )
    gather = Gather(held, (send, recv), chips, rows)
    held[z, pl.ds(pl.multiple_of(c * rows, 16), rows)] = rms_rows(tok[...], gain[...]).astype(BF16)
    gather.start()

    def work(chip):
        gather.both(chip)
        here = pl.ds(pl.multiple_of(chip * 2 * rows, 16), 2 * rows)
        bc_out[here] = jnp.dot(held[chip], w_bc[...], preferred_element_type=F32).astype(BF16)
        dt_out[here] = jnp.dot(held[chip], w_dt[...], preferred_element_type=F32)
        x_out[here] = jnp.dot(held[chip], w_x[...], preferred_element_type=F32).astype(BF16)
        z_out[here] = jnp.dot(held[chip], w_z[...], preferred_element_type=F32)

    work(z)

    @pl.loop(0, chips - 1)
    def _(step):
        gather.arrive(step)

        @pl.loop(0, 2)
        def _(side):
            chip = z + (1 + step) * (2 * side - 1)

            @pl.when((chip >= 0) & (chip < chips))
            def _():
                work(chip)

    gather.finish()


def project(tokens, gain, w_z, w_x, w_bc, w_dt, chips):
    rows = tokens.shape[0]
    total = rows * chips * 2
    spec = pl.BlockSpec(memory_space=pltpu.VMEM)
    return pl.pallas_call(
        functools.partial(project_kernel, chips, rows),
        out_shape=(
            jax.ShapeDtypeStruct((total, w_z.shape[1]), F32),
            jax.ShapeDtypeStruct((total, w_x.shape[1]), BF16),
            jax.ShapeDtypeStruct((total, w_bc.shape[1]), BF16),
            jax.ShapeDtypeStruct((total, w_dt.shape[1]), F32),
        ),
        in_specs=[spec] * 6,
        out_specs=(spec,) * 4,
        scratch_shapes=[
            pltpu.VMEM((chips, 2 * rows, tokens.shape[1]), BF16),
            pltpu.SemaphoreType.DMA((3, chips)),
            pltpu.SemaphoreType.DMA((3, chips)),
        ],
        compiler_params=pltpu.CompilerParams(
            collective_id=0, has_side_effects=True, vmem_limit_bytes=VMEM_LIMIT
        ),
        name="project",
    )(tokens, gain, w_z, w_x, w_bc, w_dt)


def scan_kernel(heads, x_ref, bc_ref, z_ref, dt_ref, dtr_ref, cum_ref, cumr_ref, skip_ref, gain_ref,
                start_ref, out_ref, sq_ref, state, scaled, gated):
    @pl.when(pl.program_id(0) == 0)
    def _():
        state[...] = start_ref[...]

    length = x_ref.shape[0]
    b_mat = bc_ref[:, :STATE_DIM]
    c_mat = bc_ref[:, STATE_DIM:]
    contract_last = (((1,), (1,)), ((), ()))
    scores = lax.dot_general(c_mat, b_mat, contract_last, preferred_element_type=F32)
    carried = lax.dot_general(c_mat, state[...].astype(BF16), contract_last, preferred_element_type=F32)
    row = lax.broadcasted_iota(jnp.int32, (length, length), 0)
    col = lax.broadcasted_iota(jnp.int32, (length, length), 1)
    causal = row >= col
    for h in range(heads):
        lanes = slice(h * HEAD_DIM, (h + 1) * HEAD_DIM)
        cum = cum_ref[:, h : h + 1]
        cum_row = cumr_ref[h : h + 1, :]
        last = cumr_ref[h : h + 1, length - 1 : length]
        weight = jnp.exp(jnp.where(causal, cum - cum_row, -1e30))
        mixed = (scores * weight * dtr_ref[h : h + 1, :]).astype(BF16)
        x_head = x_ref[:, lanes]
        x_wide = x_head.astype(F32)
        y = jnp.dot(mixed, x_head, preferred_element_type=F32)
        y = y + jnp.exp(cum) * carried[:, lanes] + skip_ref[:, lanes] * x_wide
        gated[:, lanes] = y * silu(z_ref[:, lanes])
        scaled[:, lanes] = (x_wide * (jnp.exp(last - cum) * dt_ref[:, h : h + 1])).astype(BF16)
        state[lanes, :] = state[lanes, :] * jnp.exp(last)
    state[...] += lax.dot_general(
        scaled[...], b_mat, (((0,), (0,)), ((), ())), preferred_element_type=F32
    )
    g = gated[...]
    out_ref[...] = (g * gain_ref[...]).astype(BF16)
    sq_ref[...] = lax.dot_general(
        jnp.ones((8, g.shape[1]), F32), g * g, contract_last,
        preferred_element_type=F32, precision=lax.Precision.HIGHEST,
    )


def scan(x, bc, z, dt, cum, skip, gain, start):
    total, channels = x.shape
    heads = dt.shape[1]
    by_row = lambda width: pl.BlockSpec((BLOCK_LEN, width), lambda i: (i, 0))
    by_col = lambda height: pl.BlockSpec((height, BLOCK_LEN), lambda i: (0, i))
    whole = lambda shape: pl.BlockSpec(shape, lambda i: (0, 0))
    return pl.pallas_call(
        functools.partial(scan_kernel, heads),
        grid=(total // BLOCK_LEN,),
        out_shape=(
            jax.ShapeDtypeStruct((total, channels), BF16),
            jax.ShapeDtypeStruct((8, total), F32),
        ),
        in_specs=[
            by_row(channels), by_row(bc.shape[1]), by_row(channels), by_row(heads), by_col(heads),
            by_row(heads), by_col(heads), whole((1, channels)), whole((1, channels)),
            whole((channels, STATE_DIM)),
        ],
        out_specs=(by_row(channels), by_col(8)),
        scratch_shapes=[
            pltpu.VMEM((channels, STATE_DIM), F32),
            pltpu.VMEM((BLOCK_LEN, channels), BF16),
            pltpu.VMEM((BLOCK_LEN, channels), F32),
        ],
        compiler_params=pltpu.CompilerParams(vmem_limit_bytes=VMEM_LIMIT),
        name="scan",
    )(x, bc, z, dt, dt.T, cum, cum.T, skip, gain, start)


PIECES = 4


def layer_kernel(
    chips, rows, g_ref, sq_ref, tok, gain, w_out, w_gate, w_up, w_down, out,
    part, sib, chain, held, part2, sib2, chain2, squares, resid, hidden,
    sq_send, sq_recv, sib_send, sib_recv, ch_send, ch_recv, ag_send, ag_recv,
    sib2_send, sib2_recv, ch2_send, ch2_recv,
):
    me, z, c = place()
    count = 2 * chips
    width = tok.shape[1]
    tile = width // PIECES
    other = z * 2 + 1 - c
    greet([(me != peer, jnp.int32(peer)) for peer in range(count)], count - 1)

    def sq_copy(src, slot, peer):
        return remote(sq_ref.at[src], squares.at[slot], sq_send.at[src], sq_recv.at[slot], peer)

    @pl.loop(0, count)
    def _(peer):
        @pl.when(peer != me)
        def _():
            sq_copy(peer, me, peer).start()

    def mine(ref, chip, core):
        return ref.at[chip, pl.ds(pl.multiple_of(core * rows, 16), rows)]

    def own_rows():
        return pl.ds(pl.multiple_of(c * rows, 16), rows)

    def swap(chip):
        return remote(mine(part, chip, 1 - c), sib.at[chip], sib_send.at[chip], sib_recv.at[chip], other)

    def product(chip):
        here = pl.ds(pl.multiple_of(chip * 2 * rows, 16), 2 * rows)

        @pl.loop(0, PIECES)
        def _(k):
            cols = pl.ds(pl.multiple_of(k * tile, 128), tile)
            part[chip, :, cols] = jnp.dot(
                g_ref[here], w_out[:, cols], preferred_element_type=F32
            ).astype(BF16)

        swap(chip).start()

    def move(way, chip, step):
        peer = me + 2 - 4 * way
        return remote(mine(part, chip, c), chain.at[way, step], ch_send.at[way, step], ch_recv.at[way, step], peer)

    def add(chip, way, step, use_chain):
        @pl.loop(0, PIECES)
        def _(k):
            cols = pl.ds(pl.multiple_of(k * tile, 128), tile)
            value = part[chip, own_rows(), cols].astype(F32)
            if use_chain:
                value = value + chain[way, step, :, cols].astype(F32)
            else:
                value = value + sib[chip, :, cols].astype(F32)
            part[chip, own_rows(), cols] = value.astype(BF16)

    def ends(way):
        return (z, z < chips - 1) if way == 0 else (chips - 1 - z, z > 0)

    def target(way, step):
        return chips - 1 + z - step if way == 0 else step + z - (chips - 1)

    @pl.loop(0, chips - 1)
    def _(step):
        for way in (0, 1):
            behind, more = ends(way)

            @pl.when((behind <= step) & more)
            def _():
                product(target(way, step))

        for way in (0, 1):
            behind, more = ends(way)
            chip = target(way, step)

            @pl.when((behind <= step) & more)
            def _():
                swap(chip).wait_recv()
                add(chip, way, step, False)

                @pl.when(behind > 0)
                def _():
                    move(way, chip, step - 1).wait_recv()
                    add(chip, way, step - 1, True)

                move(way, chip, step).start()

    product(z)

    @pl.loop(0, count)
    def _(peer):
        @pl.when(peer != me)
        def _():
            sq_copy(peer, peer, peer).wait_recv()

    squares[me] = sq_ref[me]
    total_sq = squares[0]
    for peer in range(1, count):
        total_sq = total_sq + squares[peer]
    row = lax.broadcasted_iota(jnp.int32, (rows, rows), 0)
    col = lax.broadcasted_iota(jnp.int32, (rows, rows), 1)
    as_column = jnp.sum(jnp.where(row == col, total_sq[0:1], 0.0), axis=1, keepdims=True)
    scale = lax.rsqrt(as_column / (HEADS * HEAD_DIM) + EPS)

    swap(z).wait_recv()
    add(z, 0, 0, False)
    for way in (0, 1):
        behind, more = ends(way)

        @pl.when(behind > 0)
        def _():
            move(way, z, chips - 2).wait_recv()
            add(z, way, chips - 2, True)

    value = (tok[...].astype(F32) + part[z, own_rows()].astype(F32) * scale).astype(BF16)
    resid[...] = value
    held[z, own_rows()] = rms_rows(value, gain[...]).astype(BF16)

    gather = Gather(held, (ag_send, ag_recv), chips, rows)
    gather.start()

    def swap2(chip):
        return remote(mine(part2, chip, 1 - c), sib2.at[chip], sib2_send.at[chip], sib2_recv.at[chip], other)

    def mlp(chip):
        gather.both(chip)
        gate = jnp.dot(held[chip], w_gate[...], preferred_element_type=F32)
        up = jnp.dot(held[chip], w_up[...], preferred_element_type=F32)
        hidden[...] = (silu(gate) * up).astype(BF16)

        @pl.loop(0, PIECES)
        def _(k):
            cols = pl.ds(pl.multiple_of(k * tile, 128), tile)
            part2[chip, :, cols] = jnp.dot(
                hidden[...], w_down[:, cols], preferred_element_type=F32
            ).astype(BF16)

        swap2(chip).start()

    def move2(way, chip, k):
        peer = me + 2 - 4 * way
        cols = pl.ds(pl.multiple_of(k * tile, 128), tile)
        return remote(
            part2.at[chip, own_rows(), cols], chain2.at[way, chip, :, cols],
            ch2_send.at[way, chip, k], ch2_recv.at[way, chip, k], peer,
        )

    def pass_on(step):
        for way in (0, 1):
            behind, more = ends(way)
            chip = step + 1 if way == 0 else chips - 2 - step
            before = (z < chip) if way == 0 else (z > chip)

            @pl.when(before)
            def _():
                swap2(chip).wait_recv()

                @pl.loop(0, PIECES)
                def _(k):
                    cols = pl.ds(pl.multiple_of(k * tile, 128), tile)
                    part2[chip, own_rows(), cols] = (
                        part2[chip, own_rows(), cols].astype(F32) + sib2[chip, :, cols].astype(F32)
                    ).astype(BF16)

                    @pl.when(behind > 0)
                    def _():
                        move2(way, chip, k).wait_recv()
                        part2[chip, own_rows(), cols] = (
                            part2[chip, own_rows(), cols].astype(F32)
                            + chain2[way, chip, :, cols].astype(F32)
                        ).astype(BF16)

                    move2(way, chip, k).start()

    mlp(z)

    @pl.loop(0, chips - 1)
    def _(step):
        gather.arrive(step)

        @pl.loop(0, 2)
        def _(side):
            chip = z + (1 + step) * (2 * side - 1)

            @pl.when((chip >= 0) & (chip < chips))
            def _():
                mlp(chip)

        @pl.when(step > 0)
        def _():
            pass_on(step - 1)

    pass_on(chips - 2)

    swap2(z).wait_recv()

    @pl.loop(0, PIECES)
    def _(k):
        cols = pl.ds(pl.multiple_of(k * tile, 128), tile)
        part2[z, own_rows(), cols] = (
            part2[z, own_rows(), cols].astype(F32) + sib2[z, :, cols].astype(F32)
        ).astype(BF16)
        for way in (0, 1):
            behind, more = ends(way)

            @pl.when(behind > 0)
            def _():
                move2(way, z, k).wait_recv()
                part2[z, own_rows(), cols] = (
                    part2[z, own_rows(), cols].astype(F32) + chain2[way, z, :, cols].astype(F32)
                ).astype(BF16)

        out[:, cols] = (
            resid[:, cols].astype(F32) + part2[z, own_rows(), cols].astype(F32)
        ).astype(BF16)

    gather.finish()

    @pl.loop(0, count)
    def _(peer):
        @pl.when(peer != me)
        def _():
            sq_copy(peer, me, peer).wait_send()

    @pl.loop(0, chips)
    def _(chip):
        swap(chip).wait_send()
        swap2(chip).wait_send()

    @pl.loop(0, chips - 1)
    def _(step):
        for way in (0, 1):
            behind, more = ends(way)
            chip = step + 1 if way == 0 else chips - 2 - step
            before = (z < chip) if way == 0 else (z > chip)

            @pl.when((behind <= step) & more)
            def _():
                move(way, target(way, step), step).wait_send()

            @pl.when(before)
            def _():
                @pl.loop(0, PIECES)
                def _(k):
                    move2(way, chip, k).wait_send()


def layer(g, sq, tokens, gain, w_out, w_gate, w_up, w_down, chips):
    rows, width = tokens.shape
    spec = pl.BlockSpec(memory_space=pltpu.VMEM)
    dma = pltpu.SemaphoreType.DMA
    return pl.pallas_call(
        functools.partial(layer_kernel, chips, rows),
        out_shape=jax.ShapeDtypeStruct((rows, width), BF16),
        in_specs=[spec] * 8,
        out_specs=spec,
        scratch_shapes=[
            pltpu.VMEM((chips, 2 * rows, width), BF16),
            pltpu.VMEM((chips, rows, width), BF16),
            pltpu.VMEM((2, chips - 1, rows, width), BF16),
            pltpu.VMEM((chips, 2 * rows, width), BF16),
            pltpu.VMEM((chips, 2 * rows, width), BF16),
            pltpu.VMEM((chips, rows, width), BF16),
            pltpu.VMEM((2, chips, rows, width), BF16),
            pltpu.VMEM((2 * chips, 8, rows), F32),
            pltpu.VMEM((rows, width), BF16),
            pltpu.VMEM((2 * rows, w_gate.shape[1]), BF16),
            dma((2 * chips,)), dma((2 * chips,)),
            dma((chips,)), dma((chips,)),
            dma((2, chips - 1)), dma((2, chips - 1)),
            dma((3, chips)), dma((3, chips)),
            dma((chips,)), dma((chips,)),
            dma((2, chips, PIECES)), dma((2, chips, PIECES)),
        ],
        compiler_params=pltpu.CompilerParams(
            collective_id=1, has_side_effects=True, vmem_limit_bytes=VMEM_LIMIT
        ),
        name="mixer_out_and_mlp",
    )(g, sq, tokens, gain, w_out, w_gate, w_up, w_down)


def local(
    tokens, norm1_gain, w_z, w_x, w_bc, w_dt, dt_bias, a_log, conv_x, conv_bc, d_skip, ssm_gain,
    w_out, norm2_gain, w_gate, w_up, w_down,
):
    count = lax.axis_size("tp")
    chips = count // 2
    rows = tokens.shape[0]
    heads = w_dt.shape[1]
    gate_z, inner_rows, bc_rows, dt_raw = project(
        tokens, norm1_gain[None], w_z, w_x, w_bc, w_dt, chips
    )
    group_len = inner_rows.shape[0]
    blocks = group_len // BLOCK_LEN
    rim = from_behind(jnp.concatenate([inner_rows[-3:], bc_rows[-3:]], axis=1), "ctx", 1)
    rim_inner, rim_bc = rim[:, : inner_rows.shape[1]], rim[:, inner_rows.shape[1] :]
    conv_inner = jax.nn.silu(conv_four(rim_inner, inner_rows, conv_x)).astype(BF16)
    conv_bcm = jax.nn.silu(conv_four(rim_bc, bc_rows, conv_bc)).astype(BF16)
    dt_step = jax.nn.softplus(dt_raw + dt_bias)
    log_decay = -dt_step * jnp.exp(a_log)
    cum = jnp.cumsum(log_decay.reshape(blocks, BLOCK_LEN, heads), axis=1)
    block_last = cum[:, -1, :]
    later = jnp.cumsum(block_last[::-1], axis=0)[::-1] - block_last
    tail = jnp.exp((block_last + later)[:, None] - cum) * dt_step.reshape(cum.shape)
    spread = jnp.repeat(jnp.eye(heads, dtype=F32), HEAD_DIM, axis=1)
    tail_wide = jnp.dot(tail.reshape(group_len, heads), spread, precision=lax.Precision.HIGHEST)
    final = lax.dot_general(
        (conv_inner.astype(F32) * tail_wide).astype(BF16),
        conv_bcm[:, :STATE_DIM],
        (((0,), (0,)), ((), ())),
        preferred_element_type=F32,
    )
    total_decay = jnp.exp(jnp.sum(block_last, axis=0))
    carried = jnp.concatenate(
        [final, jnp.broadcast_to(total_decay[:, None], (heads, STATE_DIM))], axis=0
    ).astype(BF16)
    gathered = lax.all_gather(carried, "ctx").astype(F32)
    channels = final.shape[0]
    start = jnp.zeros((heads, HEAD_DIM, STATE_DIM), F32)
    for step in range(lax.axis_size("ctx") - 1):
        fresh = gathered[step, :channels].reshape(start.shape)
        after = gathered[step, channels:][:, None, :] * start + fresh
        start = jnp.where(step < lax.axis_index("ctx"), after, start)
    gated, squares = scan(
        conv_inner, conv_bcm, gate_z, dt_step, cum.reshape(group_len, heads),
        jnp.repeat(d_skip, HEAD_DIM)[None], ssm_gain[None], start.reshape(channels, STATE_DIM),
    )
    squares = squares.reshape(8, count, rows).transpose(1, 0, 2)
    return layer(gated, squares, tokens, norm2_gain[None], w_out, w_gate, w_up, w_down, chips)


def solution(mesh):
    return jax.shard_map(
        local,
        mesh=mesh,
        in_specs=(
            P(("ctx", "tp"), None),
            P(),
            P(None, "tp"),
            P(None, "tp"),
            P(),
            P(None, "tp"),
            P("tp"),
            P("tp"),
            P(None, "tp"),
            P(),
            P("tp"),
            P("tp"),
            P("tp", None),
            P(),
            P(None, "tp"),
            P(None, "tp"),
            P("tp", None),
        ),
        out_specs=P(("ctx", "tp"), None),
        check_vma=False,
    )
```

time: 442 us -> 282 us (0.64); the launches traced: 435 us -> 281 us
  Pallas kernels: 0 us -> 242 us
  waiting for transfers between devices: 232 us -> 0.01 us
  matrix products: 79.5 us -> 2.95 us
  other arithmetic: 39 us -> 6.58 us
  blocking collectives: 34.5 us -> 12.6 us
  local copies, waits for them, and re-layouts: 27.7 us -> 13 us
  between operations: 14.5 us -> 0.38 us
    pallas_call x0 -> x3, Pallas kernels: none -> 242 us  [the longest x1 165 us: layer(): pl.pallas_call(functools.partial(layer_kernel, chips, rows), out_shape=ja...]
    reduce_scatter x2 -> x0, waiting for transfers between devices: 122 us -> none  [the longest x1 62.8 us: local(): lax.psum_scatter(jnp.dot(piece, w_out, preferred_element_type=jnp.float32...]
    all_gather x2 -> x0, waiting for transfers between devices: 109 us -> none  [the longest x1 54.8 us: local(): gathered = lax.all_gather(tokens, 'tp', axis=0, tiled=True)]
    dot_general x11 -> x2, matrix products: 79.5 us -> 2.95 us  [the longest x1 2.4 us: local(): jnp.dot(tail.reshape(group_len, heads), spread, precision=lax.Precision.H...]
    psum x1 -> x0, blocking collectives: 13.6 us -> none  [local(): squares = lax.psum(jnp.sum(gated * gated, axis=-1), 'tp')]
    reshape x6, local copies, waits for them, and re-layouts: 11 us -> 1.22 us  [the longest x1 1.04 us: local(): cum.reshape(group_len, heads)]
    unnamed x1 -> x0, blocking collectives: 8.9 us -> none
    add x4 -> x1, other arithmetic: 7.41 us -> 0.01 us  [local(): block_last + later]
  transfers between devices with their start and end apart: 6 -> 1, of which waited for: 4 -> 0; matrix products, arithmetic and copies ran while one was open for 4% -> 3% of each run, Pallas kernels for 0% -> 0%
where the time goes in v1:
time: 282 us; the launch traced here: 281 us
  Pallas kernels  242 us (86%)
  local copies, waits for them, and re-layouts  13 us (5%)
  blocking collectives  12.6 us (4%)
  other arithmetic  6.58 us (2%)
  starting transfers between devices  3.58 us (1%)
  matrix products  2.95 us (1%)
    pallas_call x1, Pallas kernels, layer(): pl.pallas_call(functools.partial(layer_kernel, chips, rows), out_shape=ja...  165 us
    pallas_call x1, Pallas kernels, project(): pl.pallas_call(functools.partial(project_kernel, chips, rows), out_shape=...  59.2 us
    pallas_call x1, Pallas kernels, scan(): pl.pallas_call(functools.partial(scan_kernel, heads), grid=(total // BLOC...  17.8 us
    all_gather x1, blocking collectives, local(): gathered = lax.all_gather(carried, 'ctx').astype(F32)  12.6 us
  transfers between devices with their start and end apart: 1, of which 0 were waited for; matrix products, arithmetic and copies ran while one was open for 3% of the time, Pallas kernels for 0%

profile of v1, /device:TPU:0, one launch (start us, length us, event | category | flops | bytes accessed | tf_op | source)
XLA Modules:
  0.0 281.4 jit_solution(13014434751886641021)
XLA Ops:
  0.0 2.0 copy.36.w_dt
  2.0 1.3 broadcast_in_dim.29.gain
  3.3 59.2 %project.1 = (f32[1024,640]{1,0:T(8,128)}, bf16[1024,640]{1,0:T(8,128)(2,1)}, bf16[1024,256]{1,0:T(8,128)(2,1)}, f32[1024,10]{1,0:T(8,128)}) custom-call(bf16[128,2560]{1,0:T(8,128)(2,1)} %tok.3, f32[1,2560]{1,0:T(1,128)} %broadcast_in_dim.29.gain, bf16[2560,640]{1,0:T(8,128)(2,1)} %w_z.1, bf16[2560,640]{1,0:T(8,128)(2,1)} %w_x.1, bf16[2560,256]{1,0:T(8,128)(2,1)} %w_bc.1, ...), custom_call_target="tpu_custom_call" | custom-call | tf_op jit(solution)/shard_map/project/pallas_call | solution.py:174
  62.6 0.8 slice.91
  63.4 0.7 slice.92
  64.1 3.6 %collective-permute-start = (bf16[3,896]{1,0:T(4,128)(2,1)S(1)}, bf16[3,896]{1,0:T(4,128)(2,1)S(1)}, u32[]{:S(2)}, u32[]{:S(2)}) collective-permute-start(bf16[3,896]{1,0:T(4,128)(2,1)S(1)} %pad_maximum_fusion.1), channel_id=1, source_target_pairs={{0,8},{8,16},{16,24},{1,9},{9,17},{17,25},{2,10},{10,18},{18,26},{... | collective-permute-start | bytes 16136 | tf_op jit(solution)/shard_map/ppermute | solution.py:24
  67.7 1.2 copy.37
  69.1 2.3 reduce-window.6
  71.8 0.2 slice_reduce_fusion.4
  72.6 1.0 copy.44.dt_ref
  73.9 1.0 copy.45.cum_ref
  75.0 0.7 broadcast_in_dim_reshape.3.skip_ref
  75.7 0.6 broadcast_in_dim.31.gain_ref
  76.3 0.6 broadcast_in_dim.36.gain
  76.9 0.3 maximum_convert_fusion
  77.4 1.6 multiply_convert_fusion.1.x_ref
  79.0 2.4 multiply_convert_fusion
  81.4 0.6 multiply_convert_fusion.2.bc_ref
  82.0 0.6 fusion.3
  82.7 12.6 %all_gather.4 = bf16[4,650,128]{2,1,0:T(8,128)(2,1)S(1)} all-gather(bf16[1,650,128]{2,1,0:T(8,128)(2,1)S(1)} %pad_maximum_fusion), channel_id=1, replica_groups=mesh['ctx'=4,'tp'=8] {'ctx'}, dimensions={0}, use_global_device_ids=true | all-gather | bytes 832000 | tf_op jit(solution)/shard_map/all_gather | solution.py:586
  95.5 0.8 fusion.8.start_ref
  96.3 17.8 %scan.1 = (bf16[1024,640]{1,0:T(8,128)(2,1)}, f32[8,1024]{1,0:T(8,128)}) custom-call(bf16[1024,640]{1,0:T(8,128)(2,1)} %copy-done, bf16[1024,256]{1,0:T(8,128)(2,1)} %copy-done.1, f32[1024,640]{1,0:T(8,128)} %get-tuple-element.13.z_ref, f32[1024,10]{1,0:T(8,128)} %copy.44.dt_ref, f32[10,1024]{1,0:T(8,128)} %bitcast.88, f32[1024,10]{1,0:T(8,128)} %copy.45.cum_ref, ...), custom_call_target="tpu_custom_call" | custom-call | tf_op jit(solution)/shard_map/scan/pallas_call | solution.py:242
  114.1 165.3 %mixer_out_and_mlp.1 = bf16[128,2560]{1,0:T(8,128)(2,1)} custom-call(bf16[1024,640]{1,0:T(8,128)(2,1)} %get-tuple-element.15.g_ref, f32[8,8,128]{2,1,0:T(8,128)} %bitcast.97, bf16[128,2560]{1,0:T(8,128)(2,1)} %tok.3, f32[1,2560]{1,0:T(1,128)} %broadcast_in_dim.36.gain, bf16[640,2560]{1,0:T(8,128)(2,1)} %w_out.1, bf16[2560,640]{1,0:T(8,128)(2,1)} %w_gate.1, ...), custom_call_target="tpu_custom_call" | custom-call | tf_op jit(solution)/shard_map/mixer_out_and_mlp/pallas_call | solution.py:521
  279.4 2.0 copy.49
  (67 shorter events, 1.8 us)
Async XLA Ops:
  3.3 65.6 %copy-start.12 = (f32[10]{0:T(128)S(1)}, f32[10]{0:T(128)}, u32[]{:S(2)}) copy-start(f32[10]{0:T(128)} %param.24) | copy-start | bytes 124
  3.3 65.6 %copy-start.10 = (f32[10]{0:T(128)S(1)}, f32[10]{0:T(128)}, u32[]{:S(2)}) copy-start(f32[10]{0:T(128)} %param.23) | copy-start | bytes 124
  3.3 69.1 %copy-start.7 = (f32[4,640]{1,0:T(4,128)S(1)}, f32[4,640]{1,0:T(4,128)}, u32[]{:S(2)}) copy-start(f32[4,640]{1,0:T(4,128)} %param.25) | copy-start | bytes 30724
  3.3 69.1 %copy-start.8 = (f32[4,256]{1,0:T(4,128)S(1)}, f32[4,256]{1,0:T(4,128)}, u32[]{:S(2)}) copy-start(f32[4,256]{1,0:T(4,128)} %param.26) | copy-start | bytes 12292
  62.5 12.4 %copy-start.11 = (f32[10]{0:T(128)S(1)}, f32[10]{0:T(128)}, u32[]{:S(2)}) copy-start(f32[10]{0:T(128)} %param.27) | copy-start | bytes 124
  62.5 13.2 %copy-start.9 = (f32[640]{0:T(1024)S(1)}, f32[640]{0:T(1024)}, u32[]{:S(2)}) copy-start(f32[640]{0:T(1024)} %param.28) | copy-start | bytes 7684
  62.5 13.7 %copy-start.6 = (f32[2560]{0:T(1024)S(1)}, f32[2560]{0:T(1024)}, u32[]{:S(2)}) copy-start(f32[2560]{0:T(1024)} %param.30) | copy-start | bytes 30724
  62.6 14.4 %copy-start.2 = (bf16[1024,640]{1,0:T(8,128)(2,1)S(1)}, bf16[1024,640]{1,0:T(8,128)(2,1)}, u32[]{:S(2)}) copy-start(bf16[1024,640]{1,0:T(8,128)(2,1)} %get-tuple-element.11) | copy-start | bytes 3932164
  64.1 12.8 %collective-permute-start = (bf16[3,896]{1,0:T(4,128)(2,1)S(1)}, bf16[3,896]{1,0:T(4,128)(2,1)S(1)}, u32[]{:S(2)}, u32[]{:S(2)}) collective-permute-start(bf16[3,896]{1,0:T(4,128)(2,1)S(1)} %pad_maximum_fusion.1), channel_id=1, source_target_pairs={{0,8},{8,16},{16,24},{1,9},{9,17},{17,25},{2,10},{10,18},{18,26},{... | collective-permute-start | bytes 16136 | tf_op jit(solution)/shard_map/ppermute | solution.py:24
  69.0 8.2 %copy-start.3 = (f32[1024,10]{0,1:T(8,128)}, f32[1024,10]{0,1:T(8,128)S(1)}, u32[]{:S(2)}) copy-start(f32[1024,10]{0,1:T(8,128)S(1)} %get-tuple-element.22) | copy-start | bytes 122884
  73.7 3.6 %copy-start.5 = (bf16[1024,256]{1,0:T(8,128)(2,1)S(1)}, bf16[1024,256]{1,0:T(8,128)(2,1)}, u32[]{:S(2)}) copy-start(bf16[1024,256]{1,0:T(8,128)(2,1)} %get-tuple-element.12) | copy-start | bytes 1572868
  73.9 3.4 %copy-start.4 = (f32[2,8,4,256]{3,1,2,0:T(8,128)}, f32[2,8,4,256]{3,1,2,0:T(8,128)S(1)}, u32[]{:S(2)}) copy-start(f32[2,8,4,256]{3,1,2,0:T(8,128)S(1)} %copy.46) | copy-start | bytes 196612
  78.9 3.1 %copy-start = (bf16[1024,640]{1,0:T(8,128)(2,1)}, bf16[1024,640]{1,0:T(8,128)(2,1)S(1)}, u32[]{:S(2)}) copy-start(bf16[1024,640]{1,0:T(8,128)(2,1)S(1)} %multiply_convert_fusion.1.x_ref) | copy-start | bytes 3932164
  82.0 14.3 %copy-start.1 = (bf16[1024,256]{1,0:T(8,128)(2,1)}, bf16[1024,256]{1,0:T(8,128)(2,1)S(1)}, u32[]{:S(2)}) copy-start(bf16[1024,256]{1,0:T(8,128)(2,1)S(1)} %multiply_convert_fusion.2.bc_ref) | copy-start | bytes 1572868

commit v2 on v1

--- a/solution.py
+++ b/solution.py
@@ -66,18 +66,22 @@
 
 
 class Gather:
-    def __init__(self, held, sems, chips, rows):
+    def __init__(self, held, sems, chips, rows, part=0, parts=1):
         self.held, self.sems, self.chips, self.rows = held, sems, chips, rows
+        self.size = rows // parts
+        self.part = part
         self.me, self.z, self.c = place()
 
     def half(self, chip, core):
-        return self.held.at[chip, pl.ds(pl.multiple_of(core * self.rows, 16), self.rows)]
+        first = pl.multiple_of(core * self.rows + self.part * self.size, 16)
+        return self.held.at[chip, pl.ds(first, self.size)]
 
     def copy(self, kind, chip, core):
         send, recv = self.sems
         peer = (self.me + 2, self.me - 2, self.z * 2 + 1 - self.c)[kind]
         part = self.half(chip, core)
-        return remote(part, part, send.at[kind, chip], recv.at[kind, chip], peer)
+        slot = self.part * 3 + kind
+        return remote(part, part, send.at[slot, chip], recv.at[slot, chip], peer)
 
     def start(self):
         @pl.when(self.z < self.chips - 1)
@@ -263,6 +267,7 @@
 
 
 PIECES = 4
+HALVES = 2
 
 
 def layer_kernel(
@@ -308,26 +313,55 @@
 
         swap(chip).start()
 
-    def move(way, chip, step):
+    size = rows // HALVES
+
+    def some(h):
+        return pl.ds(pl.multiple_of(c * rows + h * size, 16), size)
+
+    def move(h, way, chip, step):
         peer = me + 2 - 4 * way
-        return remote(mine(part, chip, c), chain.at[way, step], ch_send.at[way, step], ch_recv.at[way, step], peer)
-
-    def add(chip, way, step, use_chain):
+        slot = way * HALVES + h
+        return remote(
+            part.at[chip, some(h)], chain.at[way, step, pl.ds(h * size, size)],
+            ch_send.at[slot, step], ch_recv.at[slot, step], peer,
+        )
+
+    def add(h, chip, way, step, use_chain):
         @pl.loop(0, PIECES)
         def _(k):
             cols = pl.ds(pl.multiple_of(k * tile, 128), tile)
-            value = part[chip, own_rows(), cols].astype(F32)
+            value = part[chip, some(h), cols].astype(F32)
             if use_chain:
-                value = value + chain[way, step, :, cols].astype(F32)
+                value = value + chain[way, step, pl.ds(h * size, size), cols].astype(F32)
             else:
-                value = value + sib[chip, :, cols].astype(F32)
-            part[chip, own_rows(), cols] = value.astype(BF16)
+                value = value + sib[chip, pl.ds(h * size, size), cols].astype(F32)
+            part[chip, some(h), cols] = value.astype(BF16)
 
     def ends(way):
         return (z, z < chips - 1) if way == 0 else (chips - 1 - z, z > 0)
 
     def target(way, step):
         return chips - 1 + z - step if way == 0 else step + z - (chips - 1)
+
+    gathers = [Gather(held, (ag_send, ag_recv), chips, rows, h, HALVES) for h in range(HALVES)]
+
+    def forward(h, step):
+        for way in (0, 1):
+            behind, more = ends(way)
+            chip = target(way, step)
+
+            @pl.when((behind <= step) & more)
+            def _():
+                if h == 0:
+                    swap(chip).wait_recv()
+                add(h, chip, way, step, False)
+
+                @pl.when(behind > 0)
+                def _():
+                    move(h, way, chip, step - 1).wait_recv()
+                    add(h, chip, way, step - 1, True)
+
+                move(h, way, chip, step).start()
 
     @pl.loop(0, chips - 1)
     def _(step):
@@ -338,21 +372,7 @@
             def _():
                 product(target(way, step))
 
-        for way in (0, 1):
-            behind, more = ends(way)
-            chip = target(way, step)
-
-            @pl.when((behind <= step) & more)
-            def _():
-                swap(chip).wait_recv()
-                add(chip, way, step, False)
-
-                @pl.when(behind > 0)
-                def _():
-                    move(way, chip, step - 1).wait_recv()
-                    add(chip, way, step - 1, True)
-
-                move(way, chip, step).start()
+        forward(0, step)
 
     product(z)
 
@@ -371,28 +391,40 @@
     as_column = jnp.sum(jnp.where(row == col, total_sq[0:1], 0.0), axis=1, keepdims=True)
     scale = lax.rsqrt(as_column / (HEADS * HEAD_DIM) + EPS)
 
+    def settle(h):
+        add(h, z, 0, 0, False)
+        for way in (0, 1):
+            behind, more = ends(way)
+
+            @pl.when(behind > 0)
+            def _():
+                move(h, way, z, chips - 2).wait_recv()
+                add(h, z, way, chips - 2, True)
+
+        here = slice(h * size, (h + 1) * size)
+        value = tok[here].astype(F32) + part[z, some(h)].astype(F32) * scale[here]
+        value = value.astype(BF16)
+        resid[here] = value
+        held[z, some(h)] = rms_rows(value, gain[...]).astype(BF16)
+        gathers[h].start()
+
     swap(z).wait_recv()
-    add(z, 0, 0, False)
-    for way in (0, 1):
-        behind, more = ends(way)
-
-        @pl.when(behind > 0)
-        def _():
-            move(way, z, chips - 2).wait_recv()
-            add(z, way, chips - 2, True)
-
-    value = (tok[...].astype(F32) + part[z, own_rows()].astype(F32) * scale).astype(BF16)
-    resid[...] = value
-    held[z, own_rows()] = rms_rows(value, gain[...]).astype(BF16)
-
-    gather = Gather(held, (ag_send, ag_recv), chips, rows)
-    gather.start()
+    settle(0)
+    for h in range(1, HALVES):
+
+        @pl.loop(0, chips - 1)
+        def _(step):
+            forward(h, step)
+            gathers[h - 1].arrive(step)
+
+        settle(h)
 
     def swap2(chip):
         return remote(mine(part2, chip, 1 - c), sib2.at[chip], sib2_send.at[chip], sib2_recv.at[chip], other)
 
     def mlp(chip):
-        gather.both(chip)
+        for gather in gathers:
+            gather.both(chip)
         gate = jnp.dot(held[chip], w_gate[...], preferred_element_type=F32)
         up = jnp.dot(held[chip], w_up[...], preferred_element_type=F32)
         hidden[...] = (silu(gate) * up).astype(BF16)
@@ -445,7 +477,7 @@
 
     @pl.loop(0, chips - 1)
     def _(step):
-        gather.arrive(step)
+        gathers[-1].arrive(step)
 
         @pl.loop(0, 2)
         def _(side):
@@ -483,7 +515,8 @@
             resid[:, cols].astype(F32) + part2[z, own_rows(), cols].astype(F32)
         ).astype(BF16)
 
-    gather.finish()
+    for gather in gathers:
+        gather.finish()
 
     @pl.loop(0, count)
     def _(peer):
@@ -505,7 +538,8 @@
 
             @pl.when((behind <= step) & more)
             def _():
-                move(way, target(way, step), step).wait_send()
+                for h in range(HALVES):
+                    move(h, way, target(way, step), step).wait_send()
 
             @pl.when(before)
             def _():
@@ -536,8 +570,8 @@
             pltpu.VMEM((2 * rows, w_gate.shape[1]), BF16),
             dma((2 * chips,)), dma((2 * chips,)),
             dma((chips,)), dma((chips,)),
-            dma((2, chips - 1)), dma((2, chips - 1)),
-            dma((3, chips)), dma((3, chips)),
+            dma((2 * HALVES, chips - 1)), dma((2 * HALVES, chips - 1)),
+            dma((3 * HALVES, chips)), dma((3 * HALVES, chips)),
             dma((chips,)), dma((chips,)),
             dma((2, chips, PIECES)), dma((2, chips, PIECES)),
         ],

time: 282 us -> 280 us (level)
  no operation moved by 1% of the time
where the time goes in v2:
time: 280 us
  Pallas kernels  241 us (86%)
  local copies, waits for them, and re-layouts  13 us (5%)
  blocking collectives  12.6 us (4%)
  other arithmetic  6.58 us (2%)
  starting transfers between devices  3.58 us (1%)
  matrix products  2.95 us (1%)
    pallas_call x1, Pallas kernels, layer(): pl.pallas_call(functools.partial(layer_kernel, chips, rows), out_shape=ja...  163 us
    pallas_call x1, Pallas kernels, project(): pl.pallas_call(functools.partial(project_kernel, chips, rows), out_shape=...  59.2 us
    pallas_call x1, Pallas kernels, scan(): pl.pallas_call(functools.partial(scan_kernel, heads), grid=(total // BLOC...  17.8 us
    all_gather x1, blocking collectives, local(): gathered = lax.all_gather(carried, 'ctx').astype(F32)  12.6 us
  transfers between devices with their start and end apart: 1, of which 0 were waited for; matrix products, arithmetic and copies ran while one was open for 3% of the time, Pallas kernels for 0%

profile of v2, /device:TPU:0, one launch (start us, length us, event | category | flops | bytes accessed | tf_op | source)
XLA Modules:
  0.0 279.6 jit_solution(11320566713544290081)
XLA Ops:
  0.0 2.0 copy.36.w_dt
  2.0 1.3 broadcast_in_dim.29.gain
  3.3 59.2 %project.1 = (f32[1024,640]{1,0:T(8,128)}, bf16[1024,640]{1,0:T(8,128)(2,1)}, bf16[1024,256]{1,0:T(8,128)(2,1)}, f32[1024,10]{1,0:T(8,128)}) custom-call(bf16[128,2560]{1,0:T(8,128)(2,1)} %tok.3, f32[1,2560]{1,0:T(1,128)} %broadcast_in_dim.29.gain, bf16[2560,640]{1,0:T(8,128)(2,1)} %w_z.1, bf16[2560,640]{1,0:T(8,128)(2,1)} %w_x.1, bf16[2560,256]{1,0:T(8,128)(2,1)} %w_bc.1, ...), custom_call_target="tpu_custom_call" | custom-call | tf_op jit(solution)/shard_map/project/pallas_call | solution.py:178
  62.6 0.8 slice.91
  63.4 0.7 slice.92
  64.1 3.6 %collective-permute-start = (bf16[3,896]{1,0:T(4,128)(2,1)S(1)}, bf16[3,896]{1,0:T(4,128)(2,1)S(1)}, u32[]{:S(2)}, u32[]{:S(2)}) collective-permute-start(bf16[3,896]{1,0:T(4,128)(2,1)S(1)} %pad_maximum_fusion.1), channel_id=1, source_target_pairs={{0,8},{8,16},{16,24},{1,9},{9,17},{17,25},{2,10},{10,18},{18,26},{... | collective-permute-start | bytes 16136 | tf_op jit(solution)/shard_map/ppermute | solution.py:24
  67.7 1.2 copy.37
  69.1 2.3 reduce-window.6
  71.8 0.2 slice_reduce_fusion.4
  72.6 1.0 copy.44.dt_ref
  73.9 1.0 copy.45.cum_ref
  75.0 0.7 broadcast_in_dim_reshape.3.skip_ref
  75.7 0.6 broadcast_in_dim.31.gain_ref
  76.3 0.6 broadcast_in_dim.36.gain
  76.9 0.3 maximum_convert_fusion
  77.4 1.6 multiply_convert_fusion.1.x_ref
  79.0 2.4 multiply_convert_fusion
  81.4 0.6 multiply_convert_fusion.2.bc_ref
  82.0 0.6 fusion.3
  82.7 12.6 %all_gather.4 = bf16[4,650,128]{2,1,0:T(8,128)(2,1)S(1)} all-gather(bf16[1,650,128]{2,1,0:T(8,128)(2,1)S(1)} %pad_maximum_fusion), channel_id=1, replica_groups=mesh['ctx'=4,'tp'=8] {'ctx'}, dimensions={0}, use_global_device_ids=true | all-gather | bytes 832000 | tf_op jit(solution)/shard_map/all_gather | solution.py:620
  95.5 0.8 fusion.8.start_ref
  96.3 17.8 %scan.1 = (bf16[1024,640]{1,0:T(8,128)(2,1)}, f32[8,1024]{1,0:T(8,128)}) custom-call(bf16[1024,640]{1,0:T(8,128)(2,1)} %copy-done, bf16[1024,256]{1,0:T(8,128)(2,1)} %copy-done.1, f32[1024,640]{1,0:T(8,128)} %get-tuple-element.13.z_ref, f32[1024,10]{1,0:T(8,128)} %copy.44.dt_ref, f32[10,1024]{1,0:T(8,128)} %bitcast.88, f32[1024,10]{1,0:T(8,128)} %copy.45.cum_ref, ...), custom_call_target="tpu_custom_call" | custom-call | tf_op jit(solution)/shard_map/scan/pallas_call | solution.py:246
  114.1 163.5 %mixer_out_and_mlp.1 = bf16[128,2560]{1,0:T(8,128)(2,1)} custom-call(bf16[1024,640]{1,0:T(8,128)(2,1)} %get-tuple-element.15.g_ref, f32[8,8,128]{2,1,0:T(8,128)} %bitcast.97, bf16[128,2560]{1,0:T(8,128)(2,1)} %tok.3, f32[1,2560]{1,0:T(1,128)} %broadcast_in_dim.36.gain, bf16[640,2560]{1,0:T(8,128)(2,1)} %w_out.1, bf16[2560,640]{1,0:T(8,128)(2,1)} %w_gate.1, ...), custom_call_target="tpu_custom_call" | custom-call | tf_op jit(solution)/shard_map/mixer_out_and_mlp/pallas_call | solution.py:555
  277.6 2.0 copy.49
  (67 shorter events, 1.8 us)
Async XLA Ops:
  3.3 65.6 %copy-start.12 = (f32[10]{0:T(128)S(1)}, f32[10]{0:T(128)}, u32[]{:S(2)}) copy-start(f32[10]{0:T(128)} %param.24) | copy-start | bytes 124
  3.3 65.6 %copy-start.10 = (f32[10]{0:T(128)S(1)}, f32[10]{0:T(128)}, u32[]{:S(2)}) copy-start(f32[10]{0:T(128)} %param.23) | copy-start | bytes 124
  3.3 69.1 %copy-start.7 = (f32[4,640]{1,0:T(4,128)S(1)}, f32[4,640]{1,0:T(4,128)}, u32[]{:S(2)}) copy-start(f32[4,640]{1,0:T(4,128)} %param.25) | copy-start | bytes 30724
  3.3 69.1 %copy-start.8 = (f32[4,256]{1,0:T(4,128)S(1)}, f32[4,256]{1,0:T(4,128)}, u32[]{:S(2)}) copy-start(f32[4,256]{1,0:T(4,128)} %param.26) | copy-start | bytes 12292
  62.5 12.4 %copy-start.11 = (f32[10]{0:T(128)S(1)}, f32[10]{0:T(128)}, u32[]{:S(2)}) copy-start(f32[10]{0:T(128)} %param.27) | copy-start | bytes 124
  62.5 13.2 %copy-start.9 = (f32[640]{0:T(1024)S(1)}, f32[640]{0:T(1024)}, u32[]{:S(2)}) copy-start(f32[640]{0:T(1024)} %param.28) | copy-start | bytes 7684
  62.5 13.7 %copy-start.6 = (f32[2560]{0:T(1024)S(1)}, f32[2560]{0:T(1024)}, u32[]{:S(2)}) copy-start(f32[2560]{0:T(1024)} %param.30) | copy-start | bytes 30724
  62.6 14.4 %copy-start.2 = (bf16[1024,640]{1,0:T(8,128)(2,1)S(1)}, bf16[1024,640]{1,0:T(8,128)(2,1)}, u32[]{:S(2)}) copy-start(bf16[1024,640]{1,0:T(8,128)(2,1)} %get-tuple-element.11) | copy-start | bytes 3932164
  64.1 12.8 %collective-permute-start = (bf16[3,896]{1,0:T(4,128)(2,1)S(1)}, bf16[3,896]{1,0:T(4,128)(2,1)S(1)}, u32[]{:S(2)}, u32[]{:S(2)}) collective-permute-start(bf16[3,896]{1,0:T(4,128)(2,1)S(1)} %pad_maximum_fusion.1), channel_id=1, source_target_pairs={{0,8},{8,16},{16,24},{1,9},{9,17},{17,25},{2,10},{10,18},{18,26},{... | collective-permute-start | bytes 16136 | tf_op jit(solution)/shard_map/ppermute | solution.py:24
  69.0 8.2 %copy-start.3 = (f32[1024,10]{0,1:T(8,128)}, f32[1024,10]{0,1:T(8,128)S(1)}, u32[]{:S(2)}) copy-start(f32[1024,10]{0,1:T(8,128)S(1)} %get-tuple-element.22) | copy-start | bytes 122884
  73.7 3.6 %copy-start.5 = (bf16[1024,256]{1,0:T(8,128)(2,1)S(1)}, bf16[1024,256]{1,0:T(8,128)(2,1)}, u32[]{:S(2)}) copy-start(bf16[1024,256]{1,0:T(8,128)(2,1)} %get-tuple-element.12) | copy-start | bytes 1572868
  73.9 3.4 %copy-start.4 = (f32[2,8,4,256]{3,1,2,0:T(8,128)}, f32[2,8,4,256]{3,1,2,0:T(8,128)S(1)}, u32[]{:S(2)}) copy-start(f32[2,8,4,256]{3,1,2,0:T(8,128)S(1)} %copy.46) | copy-start | bytes 196612
  78.9 3.1 %copy-start = (bf16[1024,640]{1,0:T(8,128)(2,1)}, bf16[1024,640]{1,0:T(8,128)(2,1)S(1)}, u32[]{:S(2)}) copy-start(bf16[1024,640]{1,0:T(8,128)(2,1)S(1)} %multiply_convert_fusion.1.x_ref) | copy-start | bytes 3932164
  82.0 14.3 %copy-start.1 = (bf16[1024,256]{1,0:T(8,128)(2,1)}, bf16[1024,256]{1,0:T(8,128)(2,1)S(1)}, u32[]{:S(2)}) copy-start(bf16[1024,256]{1,0:T(8,128)(2,1)S(1)} %multiply_convert_fusion.2.bc_ref) | copy-start | bytes 1572868
